TPU v7x, 256 devices: a whole 4x4x8 slice. The times are simulated.
256 devices in a mesh: group: 8 (over z), fsdp: 32 (over x, y, core).
Axes of the slice: x: 4, y: 4, z: 8, core: 2. Of those that a mesh axis runs over, the one named last changes fastest.
Arguments:
- grad_out: bfloat16 [16384, 4096], P(('group', 'fsdp')), may hold values from -6 to 6
- expert_ids: int32 [16384, 8], P(('group', 'fsdp')), may hold values from 0 to 127, all different within a row; in each aligned block of 64 rows (0 to 63, 64 to 127, ...) at most 5 rows name the same one
- gates: bfloat16 [16384, 8], P(('group', 'fsdp')), may hold values from 0.019897461 to 0.5
- hidden_saved: bfloat16 [256, 256, 5, 384], P(('group', 'fsdp')), may hold values from -0.59765625 to 0.59765625
- w_down: bfloat16 [256, 768, 2048], P(('group', 'fsdp')), may hold values from -0.21875 to 0.21875
Outputs:
- d_gate: float32 [16384, 8], P(('group', 'fsdp'))
- d_hidden: bfloat16 [256, 256, 5, 384], P(('group', 'fsdp'))
- d_weight: bfloat16 [256, 768, 2048], P(('group', 'fsdp'))
Inputs may be any that keep to these rules, and one draw needn't show every extreme that they name: `expert_ids`: each row names 8 different experts; among the rows of one device no expert is named more than 5 times, and on some device some expert is named exactly 5 times.
All inputs are finite; a program needn't handle non-finite values.
Results may differ from a plain program's by a relative error of at most 0.0049.
Values may be sent and summed in bfloat16 or wider, within the bound.
A program may use at most 128 MiB of HBM per device.

v0:
```python
import jax
import jax.numpy as jnp
from jax import lax
from jax.sharding import PartitionSpec as P


def swapped(block, axis, bit):
    count = lax.axis_size(axis)
    route = []
    for low in range(count):
        high = low | 1 << bit
        if high != low and high < count:
            route += [(low, high), (high, low)]
    return lax.ppermute(block, axis, route)


def entry_ranks(labels, classes):
    onehot = (labels[..., None] == jnp.arange(classes, dtype=jnp.int32)).astype(jnp.int32)
    before = jnp.cumsum(onehot, axis=-2) - onehot
    return jnp.sum(before * onehot, axis=-1)


def fill_slots(token_rows, token_gates, target, blocks, per_block, capacity):
    top_k = token_gates.shape[1]
    total_slots = blocks * per_block * capacity
    entries = jnp.arange(target.shape[0], dtype=jnp.int32)
    lookup = jnp.full((total_slots,), -1, jnp.int32).at[target].set(entries, mode="drop")
    lookup = lookup.reshape(blocks, per_block, 1, capacity)
    active = lookup >= 0
    chosen = jnp.where(active, lookup, 0)
    token_index = chosen // top_k
    halves = token_rows.reshape(token_rows.shape[0], 2, token_rows.shape[1] // 2)
    side_index = jnp.arange(2, dtype=jnp.int32).reshape(1, 1, 2, 1)
    picked_rows = halves[token_index, side_index]
    picked_rows = jnp.where(active[..., None], picked_rows, jnp.zeros((), token_rows.dtype))
    picked_gates = jnp.where(
        active, token_gates.reshape(-1)[chosen], jnp.zeros((), token_gates.dtype)
    )
    picked_gates = jnp.broadcast_to(picked_gates, (blocks, per_block, 2, capacity))
    picked_rows = picked_rows.reshape(blocks, 2 * per_block, capacity, token_rows.shape[1] // 2)
    return (picked_rows, picked_gates.reshape(blocks, 2 * per_block, capacity))


def local(grad_out, expert_ids, gates, hidden_saved, w_down):
    tok_dev, top_k = expert_ids.shape
    n_group = lax.axis_size("group")
    n_fsdp = lax.axis_size("fsdp")
    per_group = n_fsdp // 2
    experts = n_group * per_group
    capacity = hidden_saved.shape[2]
    half_h = hidden_saved.shape[3]
    half_d = w_down.shape[2]
    flat_ids = expert_ids.reshape(-1)
    own_ranks = entry_ranks(flat_ids, experts)
    target = flat_ids * capacity + own_ranks
    send_rows, send_gates = fill_slots(grad_out, gates, target, n_group, per_group, capacity)
    slot_rows, slot_gates = (
        lax.all_to_all(
            lax.all_to_all(send_rows, "group", split_axis=0, concat_axis=0, tiled=True),
            "fsdp",
            split_axis=1,
            concat_axis=1,
            tiled=True,
        ),
        lax.all_to_all(
            lax.all_to_all(send_gates, "group", split_axis=0, concat_axis=0, tiled=True),
            "fsdp",
            split_axis=1,
            concat_axis=1,
            tiled=True,
        ),
    )
    row_block = slot_rows.reshape(-1, half_d)
    gate_col = slot_gates.reshape(-1, 1).astype(jnp.float32)
    weight = w_down[0]
    partial_value = lax.dot_general(
        row_block, weight, (((1,), (1,)), ((), ())), preferred_element_type=jnp.float32
    )
    hidden_mine = hidden_saved[0].reshape(-1, half_h)
    hidden_other = swapped(hidden_mine, "fsdp", 0)
    parity = lax.axis_index("fsdp") % 2
    full_hidden = lax.cond(
        parity == 0,
        lambda: jnp.concatenate([hidden_mine, hidden_other], axis=1),
        lambda: jnp.concatenate([hidden_other, hidden_mine], axis=1),
    )
    hidden_wide = full_hidden.astype(jnp.float32)
    combined = partial_value + swapped(partial_value, "fsdp", 0)
    product = lax.dynamic_slice_in_dim(combined, parity * half_h, half_h, 1)
    gate_terms = jnp.sum(combined * hidden_wide, axis=1)
    d_hidden = (gate_col * product).astype(jnp.bfloat16).reshape(hidden_saved.shape)
    scaled = (gate_col * hidden_wide).astype(jnp.bfloat16)
    d_weight = lax.dot_general(
        scaled, row_block, (((0,), (0,)), ((), ())), preferred_element_type=jnp.float32
    )
    d_weight = d_weight.astype(jnp.bfloat16)[None]
    returned = lax.all_to_all(
        lax.all_to_all(
            gate_terms.reshape(n_group, n_fsdp, capacity),
            "group",
            split_axis=0,
            concat_axis=0,
            tiled=True,
        ),
        "fsdp",
        split_axis=1,
        concat_axis=1,
        tiled=True,
    )
    returned = returned.reshape(n_group, per_group, 2, capacity)
    gate_table = returned[:, :, 0]
    d_gate = gate_table.reshape(-1)[flat_ids * capacity + own_ranks].reshape(tok_dev, top_k)
    return (d_gate, d_hidden, d_weight)


def solution(mesh):
    in_specs = (
        P(("group", "fsdp"), None),
        P(("group", "fsdp"), None),
        P(("group", "fsdp"), None),
        P(("group", "fsdp"), None, None, None),
        P(("group", "fsdp"), None, None),
    )
    out_specs = (
        P(("group", "fsdp"), None),
        P(("group", "fsdp"), None, None, None),
        P(("group", "fsdp"), None, None),
    )
    return jax.shard_map(local, mesh=mesh, in_specs=in_specs, out_specs=out_specs, check_vma=False)
```

profile of v0, /device:TPU:1, one launch (start us, length us, event | category | flops | bytes accessed | tf_op | source)
XLA Modules:
  0.0 362.3 jit_solution(9364858368174480691)
XLA Ops:
  0.6 0.8 broadcast_multiply_fusion
  1.5 0.9 copy.64
  3.4 2.4 scatter_custom_fusion
  6.3 0.8 copy.77
  7.4 4.3 %gather_fusion.2 = bf16[640]{0:T(1024)(128)(2,1)S(1)} fusion(bf16[512]{0:T(512)(128)(2,1)S(1)} %reshape.187, s32[1024]{0:T(1024)S(1)} %pad_clamp_fusion), kind=kCustom, calls=%fused_computation.2 | custom fusion | bytes 5120 | tf_op jit(solution)/shard_map/gather | solution.py:37
  12.4 2.2 reshape.182
  14.6 30.0 %gather_fusion = bf16[1280,2048]{1,0:T(8,128)(2,1)} fusion(bf16[64,2,2048]{2,1,0:T(2,128)(2,1)} %reshape.182, s32[1280]{0:T(1024)S(1)} %reshape.192), kind=kCustom, calls=%fused_computation | custom fusion | bytes 10496000 | tf_op jit(solution)/shard_map/gather | solution.py:34
  44.6 9.7 %gather.14 = bf16[8,32,5,2048]{3,2,1,0:T(8,128)(2,1)} reshape(bf16[1280,2048]{1,0:T(8,128)(2,1)} %gather_fusion) | data formatting | bytes 10485760 | tf_op jit(solution)/shard_map/gather | solution.py:34
  54.3 7.5 %broadcast_select_fusion = bf16[8,32,5,2048]{3,2,1,0:T(8,128)(2,1)} fusion(bf16[8,32,5,2048]{3,2,1,0:T(8,128)(2,1)} %gather.14, pred[8,32,5]{2,1,0:T(8,128)(4,1)S(1)} %copy.69), kind=kLoop, calls=%fused_computation.6 | loop fusion | flops 2621440 | bytes 10487040 | tf_op jit(solution)/shard_map/jit(_where)/select_n | solution.py:35
  61.8 6.9 %copy.70 = bf16[8,32,5,2048]{3,1,2,0:T(8,128)(2,1)S(1)} copy(bf16[8,32,5,2048]{3,2,1,0:T(8,128)(2,1)} %broadcast_select_fusion) | data formatting | bytes 10485760 | tf_op jit(solution)/shard_map/jit(_where)/select_n | solution.py:35
  68.7 125.7 %all_to_all.30 = bf16[8,32,5,2048]{3,1,2,0:T(8,128)(2,1)S(1)} all-to-all(bf16[8,32,5,2048]{3,1,2,0:T(8,128)(2,1)S(1)} %copy.70), channel_id=1, replica_groups=mesh['group'=8,'fsdp'=32] {'group'}, dimensions={0} | all-to-all | bytes 10485760 | tf_op jit(solution)/shard_map/all_to_all | solution.py:59
  194.3 2.9 copy.71
  197.2 71.3 %all_to_all.31 = bf16[8,32,5,2048]{3,0,2,1:T(8,128)(2,1)S(1)} all-to-all(bf16[8,32,5,2048]{3,0,2,1:T(8,128)(2,1)S(1)} %copy.71), channel_id=1, replica_groups=mesh['group'=8,'fsdp'=32] {'fsdp'}, dimensions={1} | all-to-all | bytes 10485760 | tf_op jit(solution)/shard_map/all_to_all | solution.py:58
  268.6 6.4 %copy.72 = bf16[8,32,5,2048]{3,2,1,0:T(8,128)(2,1)} copy(bf16[8,32,5,2048]{3,0,2,1:T(8,128)(2,1)S(1)} %all_to_all.31) | data formatting | bytes 10485760 | tf_op jit(solution)/shard_map/all_to_all | solution.py:58
  274.9 10.0 %reshape.183 = bf16[1280,2048]{1,0:T(8,128)(2,1)} reshape(bf16[8,32,5,2048]{3,2,1,0:T(8,128)(2,1)} %copy.72) | data formatting | bytes 10485760 | tf_op jit(solution)/shard_map/reshape | solution.py:73
  284.9 8.7 %fusion.2 = f32[1280,768]{1,0:T(8,128)} fusion(bf16[1280,2048]{1,0:T(8,128)(2,1)} %reshape.183, bf16[1,768,2048]{2,1,0:T(8,128)(2,1)S(1)} %copy-done), kind=kOutput, calls=%fused_computation.12 | convolution fusion | flops 4026531840 | bytes 12320768 | tf_op jit(solution)/shard_map/dot_general | solution.py:76
  293.8 1.8 copy.73
  295.6 3.1 reshape_squeeze.6
  299.4 9.0 %all_to_all.32 = bf16[8,32,5]{1,2,0:T(8,128)(2,1)S(1)} all-to-all(bf16[8,32,5]{1,2,0:T(8,128)(2,1)S(1)} %copy.79), channel_id=1, replica_groups=mesh['group'=8,'fsdp'=32] {'group'}, dimensions={0} | all-to-all | bytes 5120 | tf_op jit(solution)/shard_map/all_to_all | solution.py:66
  309.1 5.1 %all-to-all-start.5 = ((bf16[8,32,5]{2,0,1:T(8,128)(2,1)}), bf16[8,32,5]{2,0,1:T(8,128)(2,1)S(1)}, u32[]{:S(2)}, u32[]{:S(2)}) async-start(bf16[8,32,5]{2,0,1:T(8,128)(2,1)} %copy.80), calls=%async_computation.5 | async-start | bytes 131072 | tf_op jit(solution)/shard_map/all_to_all | solution.py:65
  314.3 7.3 %all-to-all-done.5 = bf16[8,32,5]{2,0,1:T(8,128)(2,1)S(1)} async-done(((bf16[8,32,5]{2,0,1:T(8,128)(2,1)}), bf16[8,32,5]{2,0,1:T(8,128)(2,1)S(1)}, u32[]{:S(2)}, u32[]{:S(2)}) %all-to-all-start.5) | async-done | bytes 2592 | tf_op jit(solution)/shard_map/all_to_all | solution.py:65
  322.1 2.9 conditional.6
  322.1 2.9 pad_maximum_fusion
  325.1 6.3 %fusion = (f32[1280]{0:T(1024)S(1)}, f32[1280,768]{1,0:T(8,128)}) fusion(bf16[1280,768]{1,0:T(8,128)(2,1)} %get-tuple-element.43, f32[1280,768]{1,0:T(8,128)} %fusion.2, f32[1280,768]{1,0:T(8,128)} %collective-permute-done), kind=kLoop, calls=%fused_computation.9 | loop fusion | flops 3930880 | bytes 13767680 | tf_op jit(solution)/shard_map/reduce_sum | solution.py:90
  332.4 3.3 all-to-all-start.2
  335.7 9.2 %fusion.4 = bf16[1,768,2048]{2,1,0:T(8,128)(2,1)} fusion(bf16[1280,2048]{1,0:T(8,128)(2,1)} %reshape.183, bf16[1280,768]{1,0:T(8,128)(2,1)} %get-tuple-element.43, f32[1280]{0:T(1024)S(1)} %reshape.191), kind=kOutput, calls=%fused_computation.14 | convolution fusion | flops 4031053824 | bytes 10359808 | tf_op jit(solution)/shard_map/dot_general | solution.py:93
  346.1 0.8 copy.75
  346.9 3.9 %all-to-all-start.3 = ((f32[8,32,5]{2,0,1:T(8,128)}), f32[8,32,5]{2,0,1:T(8,128)S(1)}, u32[]{:S(2)}, u32[]{:S(2)}) async-start(f32[8,32,5]{2,0,1:T(8,128)} %copy.75), calls=%async_computation.3 | async-start | bytes 262144 | tf_op jit(solution)/shard_map/all_to_all | solution.py:97
  350.8 2.7 multiply_convert_fusion
  353.5 3.0 reshape.190
  356.5 2.5 copy.84
  359.3 2.3 gather_fusion.1
  (58 shorter events, 7.7 us)
Async XLA Ops:
  0.6 284.3 %copy-start = (bf16[1,768,2048]{2,1,0:T(8,128)(2,1)S(1)}, bf16[1,768,2048]{2,1,0:T(8,128)(2,1)}, u32[]{:S(2)}) copy-start(bf16[1,768,2048]{2,1,0:T(8,128)(2,1)} %param.11) | copy-start | bytes 9437188
  284.9 8.9 %copy-start.1 = (bf16[1,256,5,384]{3,1,2,0:T(8,128)(2,1)S(1)}, bf16[1,256,5,384]{3,1,2,0:T(8,128)(2,1)}, u32[]{:S(2)}) copy-start(bf16[1,256,5,384]{3,1,2,0:T(8,128)(2,1)} %param.10) | copy-start | bytes 2949124
  293.7 31.4 %collective-permute-start = (f32[1280,768]{1,0:T(8,128)}, f32[1280,768]{1,0:T(8,128)}, u32[]{:S(2)}, u32[]{:S(2)}) collective-permute-start(f32[1280,768]{1,0:T(8,128)} %fusion.2), channel_id=1, source_target_pairs={{0,1},{1,0},{2,3},{3,2},{4,5},{5,4},{6,7},{7,6},{8,9},{9,8},{10,11... | collective-permute-start | bytes 11796488 | tf_op jit(solution)/shard_map/ppermute | solution.py:14
  298.7 23.4 %collective-permute-start.1 = (bf16[1280,384]{1,0:T(8,128)(2,1)}, bf16[1280,384]{1,0:T(8,128)(2,1)}, u32[]{:S(2)}, u32[]{:S(2)}) collective-permute-start(bf16[1280,384]{1,0:T(8,128)(2,1)} %reshape_squeeze.6), channel_id=1, source_target_pairs={{0,1},{1,0},{2,3},{3,2},{4,5},{5,4},{6,7},{7,6},{8,9},{9,8},{10,11... | collective-permute-start | bytes 2949128 | tf_op jit(solution)/shard_map/ppermute | solution.py:14
  309.1 12.5 %all-to-all-start.5 = ((bf16[8,32,5]{2,0,1:T(8,128)(2,1)}), bf16[8,32,5]{2,0,1:T(8,128)(2,1)S(1)}, u32[]{:S(2)}, u32[]{:S(2)}) async-start(bf16[8,32,5]{2,0,1:T(8,128)(2,1)} %copy.80), calls=%async_computation.5 | async-start | bytes 131072 | tf_op jit(solution)/shard_map/all_to_all | solution.py:65
  332.4 12.5 %all-to-all-start.2 = ((f32[8,1,160]{2,1,0:T(1,128)}), f32[8,1,160]{2,1,0:T(1,128)S(1)}, u32[]{:S(2)}, u32[]{:S(2)}) async-start(f32[8,1,160]{2,1,0:T(1,128)} %reshape.228), calls=%async_computation.2 | async-start | bytes 16384 | tf_op jit(solution)/shard_map/all_to_all | solution.py:98
  346.9 12.1 %all-to-all-start.3 = ((f32[8,32,5]{2,0,1:T(8,128)}), f32[8,32,5]{2,0,1:T(8,128)S(1)}, u32[]{:S(2)}, u32[]{:S(2)}) async-start(f32[8,32,5]{2,0,1:T(8,128)} %copy.75), calls=%async_computation.3 | async-start | bytes 262144 | tf_op jit(solution)/shard_map/all_to_all | solution.py:97
where the time goes:
time: 364 us; the launch traced here: 362 us
  blocking collectives  206 us (57%)
  local copies, waits for them, and re-layouts  95.7 us (26%)
  other arithmetic  21.6 us (6%)
  matrix products  17.9 us (5%)
  starting transfers between devices  12.8 us (4%)
  waiting for transfers between devices  7.34 us (2%)
    all_to_all x1, blocking collectives, local(): lax.all_to_all(send_rows, 'group', split_axis=0, concat_axis=0, tiled=True)  126 us
    all_to_all x1, blocking collectives, local(): lax.all_to_all(lax.all_to_all(send_rows, 'group', split_axis=0, concat_ax...  71.3 us
    gather x2, local copies, waits for them, and re-layouts, fill_slots(): picked_rows = halves[token_index, side_index]  39.7 us
    reshape x1, local copies, waits for them, and re-layouts, local(): row_block = slot_rows.reshape(-1, half_d)  10 us
    dot_general x1, matrix products, local(): lax.dot_general(scaled, row_block, (((0,), (0,)), ((), ())), preferred_el...  9.16 us
    all_to_all x1, blocking collectives, local(): lax.all_to_all(send_gates, 'group', split_axis=0, concat_axis=0, tiled=True)  8.98 us
    dot_general x1, matrix products, local(): lax.dot_general(row_block, weight, (((1,), (1,)), ((), ())), preferred_el...  8.74 us
    select_n x1, other arithmetic, fill_slots(): jnp.where(active[..., None], picked_rows, jnp.zeros((), token_rows.dtype))  7.46 us
  transfers between devices with their start and end apart: 5, of which 1 were waited for; matrix products, arithmetic and copies ran while one was open for 7% of the time, Pallas kernels for 0%

commit v1 on v0

v1 whole, which is shorter than its diff:
```python
import jax
import jax.numpy as jnp
from jax import lax
from jax.experimental import pallas as pl
from jax.experimental.pallas import tpu as pltpu
from jax.sharding import PartitionSpec as P

MESH = pl.DeviceIdType.MESH
F32 = jnp.float32
BF16 = jnp.bfloat16

NZ, NX, NY = 8, 4, 4
NP = NX * NY
TOK, TOP = 64, 8
CAP = 5
SRC = 2 * NZ
ROWS = CAP * SRC
HALF_D, H, HALF_H = 2048, 768, 384
EXPERTS = NZ * NP
DEAD = -1000.0

WIDTHS = (256,) * 8
STARTS = tuple(sum(WIDTHS[:i]) for i in range(len(WIDTHS)))
K = len(WIDTHS)


def iota(shape, dim):
    return lax.broadcasted_iota(jnp.int32, shape, dim)


def nt(a, b):
    return lax.dot_general(a, b, (((1,), (1,)), ((), ())), preferred_element_type=F32)


def nn(a, b):
    return lax.dot_general(a, b, (((1,), (0,)), ((), ())), preferred_element_type=F32)


def wait_for(ref, sem):
    pltpu.make_async_copy(ref, ref, sem).wait()


def kernel(
    g_hbm, ids_ref, gates_ref, h_hbm, w_hbm,
    dgate_ref, dh_hbm, dw_hbm,
    tok, send, recv, pick, w_v, uacc, h_raw, h_all, scaled_t, dw_v, uex, dh_v, gate_col,
    idx_mine, idx_other, meta_s, meta_r, code, gate_g, gm_s, gm_r, gp_s, gp_r, g2_s, g2_r, look, zmask,
    sem_h, sem_w, sem_loc, swap_s, swap_r, idx_sem, hx_sem, meta_ss, meta_rs,
    z_s, z_r, xy_s, xy_r, gm_ss, gm_rs, ex_s, ex_r, gp_ss, gp_rs, g2_ss, g2_rs, dw_sem, dh_sem,
):
    z = lax.axis_index("group")
    f = lax.axis_index("fsdp")
    p = f // 2
    core = f % 2
    x = p // NY
    y = p % NY
    other = 1 - core

    def plane(i):
        dx, dy = i // NY, i % NY
        return ((x + dx) % NX) * NY + (y + dy) % NY

    sibling = (z, p * 2 + other)

    def remote(src, dst, ss, rs, dev):
        return pltpu.make_async_remote_copy(
            src_ref=src, dst_ref=dst, send_sem=ss, recv_sem=rs, device_id=dev, device_id_type=MESH
        )

    locals_ = []
    for k in range(K):
        cp = pltpu.make_async_copy(
            g_hbm.at[:, pl.ds(pl.multiple_of(core * HALF_D + STARTS[k], 128), WIDTHS[k])],
            tok.at[z, core, :, pl.ds(STARTS[k], WIDTHS[k])],
            sem_loc.at[k],
        )
        cp.start()
        locals_.append(cp)
    h_in = pltpu.make_async_copy(h_hbm, h_raw.at[core], sem_h)
    h_in.start()
    w_in = pltpu.make_async_copy(w_hbm, w_v, sem_w)
    w_in.start()

    barrier = pltpu.get_barrier_semaphore()
    partners = [sibling]
    for d in range(1, NZ):
        partners.append(((z + d) % NZ, f))
        partners.append(((z + d) % NZ, p * 2 + other))
    for i in range(1, NP):
        partners.append((z, plane(i) * 2 + core))
    for dev in partners:
        pl.semaphore_signal(barrier, 1, device_id=dev, device_id_type=MESH)
    pl.semaphore_wait(barrier, len(partners))

    swaps = []
    for k in range(K):
        cols = pl.ds(STARTS[k], WIDTHS[k])
        cp = remote(
            g_hbm.at[:, pl.ds(pl.multiple_of(other * HALF_D + STARTS[k], 128), WIDTHS[k])],
            tok.at[z, core, :, cols], swap_s.at[k], swap_r.at[k], sibling,
        )
        swaps.append(cp)
    swaps[0].start()

    lanes16 = iota((16, 128), 1)
    both = jnp.concatenate([ids_ref[...].astype(F32), gates_ref[...].astype(F32)], axis=0)
    twice = jnp.concatenate([both, both], axis=1)
    idx_mine[...] = jnp.where(lanes16 // TOK == core, twice, 0.0)
    idx_cp = remote(idx_mine, idx_other, idx_sem.at[0], idx_sem.at[1], sibling)
    idx_cp.start()
    for k in range(1, K):
        swaps[k].start()
    hx_cp = remote(h_hbm, h_raw.at[core], hx_sem.at[0], hx_sem.at[1], sibling)
    hx_cp.start()

    def ring(k, hop, way):
        sign = 1 if way == 0 else -1
        slot = (z - sign * (hop - 1) + 2 * NZ) % NZ
        ref = tok.at[slot, :, :, pl.ds(STARTS[k], WIDTHS[k])]
        return remote(ref, ref, z_s.at[k], z_r.at[way, hop - 1, k], ((z + sign + NZ) % NZ, f))

    def arrived(k, hop, way):
        sign = 1 if way == 0 else -1
        slot = (z - sign * hop + 2 * NZ) % NZ
        ref = tok.at[slot, :, :, pl.ds(STARTS[k], WIDTHS[k])]
        wait_for(ref, z_r.at[way, hop - 1, k])

    def hop1(k):
        locals_[k].wait()
        swaps[k].wait_recv()
        ring(k, 1, 0).start()
        ring(k, 1, 1).start()

    def hop23(k, hop):
        for way in (0, 1):
            arrived(k, hop - 1, way)
            ring(k, hop, way).start()

    def hop4(k):
        way = k % 2
        arrived(k, 3, way)
        ring(k, 4, way).start()

    def gathered(k):
        arrived(k, 3, 1 - k % 2)
        arrived(k, 4, k % 2)

    hop1(0)

    idx_cp.wait_recv()
    table = idx_mine[...] + idx_other[...]
    expert = iota((EXPERTS, 128), 0).astype(F32)
    named = jnp.zeros((EXPERTS, 128), F32)
    by_expert = jnp.zeros((EXPERTS, 128), F32)
    for k in range(TOP):
        hit = expert == table[k : k + 1]
        named = named + jnp.where(hit, 1.0, 0.0)
        by_expert = by_expert + jnp.where(hit, table[TOP + k : TOP + k + 1], 0.0)
    before = iota((128, 128), 0)
    after = iota((128, 128), 1)
    upper = jnp.where((before < after) & (before // TOK == after // TOK), 1.0, 0.0).astype(BF16)
    rank = nn(named.astype(BF16), upper)
    rank_or = jnp.where(named > 0, rank, DEAD).astype(BF16)
    meta_s[:, 0:16] = rank_or.reshape(NZ, NP, 128)
    meta_s[:, 16:32] = by_expert.astype(BF16).reshape(NZ, NP, 128)
    metas = []
    for d in range(1, NZ):
        to = (z + d) % NZ
        cp = remote(meta_s.at[to], meta_r.at[z], meta_ss.at[d - 1], meta_rs.at[d - 1], (to, f))
        cp.start()
        metas.append(cp)
    meta_r[z] = meta_s[z]

    hop1(1)
    hop23(0, 2)

    lane_l = iota((128, 128), 0)
    sub8 = iota((8, 128), 0)
    for k in range(TOP):
        ids_k = table[k : k + 1]
        rank_k = jnp.sum(jnp.where(expert == ids_k, rank, 0.0), axis=0, keepdims=True)
        ids_i = ids_k.astype(jnp.int32)
        place = (ids_i % NP) * CAP + rank_k.astype(jnp.int32)
        look[:, k * 128 : (k + 1) * 128] = jnp.where(lane_l == place, 1.0, 0.0).astype(BF16)
        zmask[:, k * 128 : (k + 1) * 128] = jnp.where(sub8 == ids_i // NP, 1.0, 0.0)

    hop1(2)
    hop23(1, 2)
    hop23(0, 3)

    for cp in metas:
        cp.wait_recv()
    for j in range(NZ):
        lane_src = (j * 128 + iota((NP, 128), 1)) // TOK
        code[:, j * 128 : (j + 1) * 128] = meta_r[j, 0:16].astype(F32) + 8.0 * lane_src.astype(F32)
        gate_g[:, j * 128 : (j + 1) * 128] = meta_r[j, 16:32]
    row = iota((ROWS, 1024), 0)
    target = (row // SRC + 8 * (row % SRC)).astype(F32)

    @pl.loop(0, NP)
    def _(e):
        chosen = jnp.where(code[pl.ds(e, 1), :] == target, 1.0, 0.0).astype(BF16)
        pick[e] = chosen
        gm = nt(gate_g[...], chosen)
        gm_s[e] = jnp.concatenate([gm, jnp.zeros((NP, 128 - ROWS), F32)], axis=1).astype(BF16)

    hop1(3)
    hop23(2, 2)
    hop23(1, 3)
    hop4(0)

    for i in range(1, NP):
        to = plane(i)
        remote(gm_s.at[to], gm_r.at[p], gm_ss, gm_rs, (z, to * 2 + core)).start()
    gm_r[p] = gm_s[p]

    def select(k):
        cols = pl.ds(STARTS[k], WIDTHS[k])
        w = WIDTHS[k]

        @pl.loop(0, NP // 4)
        def _(q):
            lhs = pick[pl.ds(q * 4, 4)].reshape(4 * ROWS, 1024)
            out = nn(lhs, tok[:, :, :, cols].reshape(1024, w))
            send[pl.ds(q * 4, 4), :, :, cols] = out.astype(BF16).reshape(4, CAP, SRC, w)

        for i in range(1, NP):
            to = plane(i)
            remote(
                send.at[to, :, :, cols], recv.at[:, p, :, cols], xy_s.at[k], xy_r.at[k],
                (z, to * 2 + core),
            ).start()
        recv[:, p, :, cols] = send[p, :, :, cols]

    r_i = iota((256, 256), 0)
    s_i = iota((256, 256), 1)
    perm = jnp.where(((r_i % 16) // 2) * 32 + (r_i // 16) * 2 + r_i % 2 == s_i, 1.0, 0.0).astype(BF16)
    back = jnp.where(((r_i % 32) // 2) * 16 + (r_i // 32) * 2 + r_i % 2 == s_i, 1.0, 0.0).astype(BF16)
    eye = jnp.where(r_i == s_i, 1.0, 0.0).astype(BF16)

    def hidden_task():
        h_in.wait()
        hx_cp.wait_recv()
        for j in range(2):
            for c in range(CAP):
                h_all[c, :, j * HALF_H : (j + 1) * HALF_H] = nn(perm, h_raw[j, c]).astype(BF16)

    def gate_task():
        wait_for(gm_r.at[pl.ds(0, NP - 1)], gm_rs)
        mine = jnp.where(iota((NP, NP, 128), 1) == p, gm_r[...].astype(F32), 0.0)
        gates = jnp.sum(mine, axis=1).astype(BF16)
        spread = jnp.where(iota((256, NP), 0) // SRC == iota((256, NP), 1), 1.0, 0.0).astype(BF16)
        wide = nn(spread, gates)
        lane = iota((256, 128), 1)
        src = iota((256, 128), 0) % SRC
        for c in range(CAP):
            col = jnp.sum(jnp.where(lane == c * SRC + src, wide, 0.0), axis=1, keepdims=True)
            gate_col[c] = jnp.broadcast_to(col, (256, 128))
            scaled = (col * h_all[c].astype(F32)).astype(BF16)
            for b in range(3):
                scaled_t[b * 256 : (b + 1) * 256, c * 256 : (c + 1) * 256] = nt(
                    eye, scaled[:, b * 256 : (b + 1) * 256]
                ).astype(BF16)

    def take_u(k):
        cols = pl.ds(STARTS[k], WIDTHS[k])
        w = WIDTHS[k]
        wait_for(recv.at[:, pl.ds(0, NP - 1), :, cols], xy_r.at[k])

        @pl.loop(0, CAP)
        def _(c):
            part = nt(recv[c, :, :, cols].reshape(256, w), w_v[:, cols])
            if k == 0:
                uacc[c] = part
            else:
                uacc[c] += part

    def take_w(k):
        cols = pl.ds(STARTS[k], WIDTHS[k])
        w = WIDTHS[k]

        @pl.loop(0, 3)
        def _(b):
            rows = pl.ds(pl.multiple_of(b * 256, 256), 256)
            out = nn(scaled_t[rows, :], recv[:, :, :, cols].reshape(5 * 256, w))
            dw_v[rows, cols] = out.astype(BF16)

        pltpu.make_async_copy(dw_v.at[:, cols], dw_hbm.at[:, cols], dw_sem.at[k]).start()

    for t in range(4, K + 6):
        if t < K:
            hop1(t)
        if t - 1 < K:
            hop23(t - 1, 2)
        if t - 2 < K:
            hop23(t - 2, 3)
        if t - 3 < K:
            hop4(t - 3)
        if t - 4 < K:
            gathered(t - 4)
            select(t - 4)
        if t == 4:
            hidden_task()
        if t == 5:
            gate_task()
            w_in.wait()
        if t >= 6:
            take_u(t - 6)
            if t - 6 < K - 1:
                take_w(t - 6)

    exs = []
    lane_t = iota((256, 128), 1)
    terms = jnp.zeros((256, 128), F32)
    for c in range(CAP):
        cp = remote(
            uacc.at[c, :, pl.ds(pl.multiple_of(other * HALF_H, 128), HALF_H)], uex.at[c],
            ex_s.at[c], ex_r.at[c], sibling,
        )
        cp.start()
        exs.append(cp)
    for c in range(CAP):
        part = jnp.sum(uacc[c] * h_all[c].astype(F32), axis=1, keepdims=True)
        terms = terms + jnp.where(lane_t == p * CAP + c, part, 0.0)
    gp_s[...] = terms.reshape(NP, SRC, 128)
    for i in range(1, NP):
        to = plane(i)
        remote(gp_s.at[to], gp_r.at[p], gp_ss, gp_rs, (z, to * 2 + core)).start()
    gp_r[p] = gp_s[p]

    take_w(K - 1)

    def finish_hidden(c):
        exs[c].wait_recv()
        u = uacc[c, :, pl.ds(pl.multiple_of(core * HALF_H, 128), HALF_H)] + uex[c]
        dh = (gate_col[c, :, 0:1] * u).astype(BF16)
        dh_v[c] = nn(back, dh).astype(BF16)
        pltpu.make_async_copy(dh_v.at[c], dh_hbm.at[c], dh_sem.at[c]).start()

    for c in range(CAP):
        finish_hidden(c)

    wait_for(gp_r.at[pl.ds(0, NP - 1)], gp_rs)
    total = jnp.sum(gp_r[...], axis=0)
    g2_s[...] = jnp.broadcast_to(total[:, None, :], (SRC, 8, 128))
    g2 = []
    for d in range(NZ):
        to = (z + d) % NZ
        for flip in (0, 1):
            if d == 0 and flip == 0:
                continue
            to_core = core if flip == 0 else other
            n = 2 * d + flip - 1
            cp = remote(
                g2_s.at[to * 2 + to_core], g2_r.at[core, z], g2_ss.at[n], g2_rs.at[n],
                (to, p * 2 + to_core),
            )
            cp.start()
            g2.append(cp)
    g2_r[core, z] = g2_s[z * 2 + core]
    for cp in g2:
        cp.wait_recv()
    summed = g2_r[0] + g2_r[1]
    zi = iota((NZ, 8, 128), 0)
    si = iota((NZ, 8, 128), 1)
    terms8 = jnp.sum(jnp.where(zi == si, summed, 0.0), axis=0)
    hi = terms8.astype(BF16)
    rest = terms8 - hi.astype(F32)
    mid = rest.astype(BF16)
    low = (rest - mid.astype(F32)).astype(BF16)
    for k in range(TOP):
        lk = look[:, k * 128 : (k + 1) * 128]
        got = nn(hi, lk) + nn(mid, lk) + nn(low, lk)
        line = jnp.sum(got * zmask[:, k * 128 : (k + 1) * 128], axis=0, keepdims=True)
        dgate_ref[k : k + 1, :] = jnp.where(core == 0, line[:, 0:TOK], line[:, TOK:])

    idx_cp.wait_send()
    hx_cp.wait_send()
    for cp in swaps + metas + exs + g2:
        cp.wait_send()
    for k in range(K):
        cols = pl.ds(STARTS[k], WIDTHS[k])
        wait_for(tok.at[pl.ds(0, NZ - 1), :, :, cols], z_s.at[k])
        wait_for(recv.at[:, pl.ds(0, NP - 1), :, cols], xy_s.at[k])
        pltpu.make_async_copy(dw_v.at[:, cols], dw_hbm.at[:, cols], dw_sem.at[k]).wait()
    for c in range(CAP):
        pltpu.make_async_copy(dh_v.at[c], dh_hbm.at[c], dh_sem.at[c]).wait()
    wait_for(gm_r.at[pl.ds(0, NP - 1)], gm_ss)
    wait_for(gp_r.at[pl.ds(0, NP - 1)], gp_ss)


def local(grad_out, expert_ids, gates, hidden_saved, w_down):
    dma = pltpu.SemaphoreType.DMA
    vm = pltpu.VMEM
    anywhere = pl.BlockSpec(memory_space=pl.ANY)
    in_vmem = pl.BlockSpec(memory_space=pltpu.VMEM)
    scratch = [
        vm((NZ, 2, TOK, HALF_D), BF16),
        vm((NP, CAP, SRC, HALF_D), BF16),
        vm((CAP, NP, SRC, HALF_D), BF16),
        vm((NP, ROWS, 1024), BF16),
        vm((H, HALF_D), BF16),
        vm((CAP, 256, H), F32),
        vm((2, CAP, 256, HALF_H), BF16),
        vm((CAP, 256, H), BF16),
        vm((H, CAP * 256), BF16),
        vm((H, HALF_D), BF16),
        vm((CAP, 256, HALF_H), F32),
        vm((CAP, 256, HALF_H), BF16),
        vm((CAP, 256, 128), F32),
        vm((16, 128), F32),
        vm((16, 128), F32),
        vm((NZ, 32, 128), BF16),
        vm((NZ, 32, 128), BF16),
        vm((NP, 1024), F32),
        vm((NP, 1024), BF16),
        vm((NP, NP, 128), BF16),
        vm((NP, NP, 128), BF16),
        vm((NP, SRC, 128), F32),
        vm((NP, SRC, 128), F32),
        vm((SRC, 8, 128), F32),
        vm((2, NZ, 8, 128), F32),
        vm((128, TOP * 128), BF16),
        vm((8, TOP * 128), F32),
        dma, dma, dma((K,)), dma((K,)), dma((K,)), dma((2,)), dma((2,)), dma((7,)), dma((7,)),
        dma((K,)), dma((2, 4, K)), dma((K,)), dma((K,)), dma, dma, dma((CAP,)), dma((CAP,)),
        dma, dma, dma((15,)), dma((15,)), dma((K,)), dma((CAP,)),
    ]
    d_gate, d_hidden, d_weight = pl.pallas_call(
        kernel,
        out_shape=(
            jax.ShapeDtypeStruct((TOP, TOK), F32),
            jax.ShapeDtypeStruct((CAP, 256, HALF_H), BF16),
            jax.ShapeDtypeStruct((H, HALF_D), BF16),
        ),
        in_specs=[anywhere, in_vmem, in_vmem, anywhere, anywhere],
        out_specs=(in_vmem, anywhere, anywhere),
        scratch_shapes=scratch,
        compiler_params=pltpu.CompilerParams(
            collective_id=0, has_side_effects=True, vmem_limit_bytes=56 * 2**20
        ),
        cost_estimate=pl.CostEstimate(
            flops=15 * 10**9, bytes_accessed=10 * 10**6, transcendentals=0
        ),
    )(grad_out, expert_ids.T, gates.T, jnp.transpose(hidden_saved[0], (1, 0, 2)), w_down[0])
    return d_gate.T, jnp.transpose(d_hidden, (1, 0, 2))[None], d_weight[None]


def solution(mesh):
    spec = P(("group", "fsdp"), None)
    in_specs = (
        spec,
        spec,
        spec,
        P(("group", "fsdp"), None, None, None),
        P(("group", "fsdp"), None, None),
    )
    out_specs = (spec, P(("group", "fsdp"), None, None, None), P(("group", "fsdp"), None, None))
    return jax.shard_map(local, mesh=mesh, in_specs=in_specs, out_specs=out_specs, check_vma=False)
```

time: 364 us -> 117 us (0.32)
  blocking collectives: 206 us -> 0 us
  Pallas kernels: 0 us -> 109 us
  local copies, waits for them, and re-layouts: 95.7 us -> 7.48 us
  other arithmetic: 21.6 us -> 0 us
  matrix products: 17.9 us -> 0 us
  starting transfers between devices: 12.8 us -> 0 us
  waiting for transfers between devices: 7.34 us -> 0 us
    all_to_all x3 -> x0, blocking collectives: 206 us -> none  [the longest x1 126 us: local(): lax.all_to_all(send_rows, 'group', split_axis=0, concat_axis=0, tiled=True)]
    pallas_call x0 -> x1, Pallas kernels: none -> 109 us  [local(): pl.pallas_call(kernel, out_shape=(jax.ShapeDtypeStruct((TOP, TOK), F32),...]
    gather x5 -> x0, local copies, waits for them, and re-layouts: 46.6 us -> none  [the longest x2 39.7 us: fill_slots(): picked_rows = halves[token_index, side_index]]
    dot_general x2 -> x0, matrix products: 17.9 us -> none  [the longest x1 9.16 us: local(): lax.dot_general(scaled, row_block, (((0,), (0,)), ((), ())), preferred_el...]
    reshape x10 -> x0, local copies, waits for them, and re-layouts: 16.2 us -> none  [the longest x1 10 us: local(): row_block = slot_rows.reshape(-1, half_d)]
    all_to_all x3 -> x0, starting transfers between devices: 12.3 us -> none  [the longest x1 5.1 us: local(): lax.all_to_all(lax.all_to_all(send_gates, 'group', split_axis=0, concat_a...]
    all_to_all x6 -> x0, local copies, waits for them, and re-layouts: 11.4 us -> none  [the longest x1 6.35 us: local(): lax.all_to_all(lax.all_to_all(send_rows, 'group', split_axis=0, concat_ax...]
    select_n x4 -> x0, other arithmetic: 7.5 us -> none  [the longest x1 7.46 us: fill_slots(): jnp.where(active[..., None], picked_rows, jnp.zeros((), token_rows.dtype))]
  transfers between devices with their start and end apart: 5 -> 0, of which waited for: 1 -> 0; matrix products, arithmetic and copies ran while one was open for 7% -> 0% of each run, Pallas kernels for 0% -> 0%
where the time goes in v1:
time: 117 us
  Pallas kernels  109 us (93%)
  local copies, waits for them, and re-layouts  7.48 us (6%)
    pallas_call x1, Pallas kernels, local(): pl.pallas_call(kernel, out_shape=(jax.ShapeDtypeStruct((TOP, TOK), F32),...  109 us
    unnamed x3, local copies, waits for them, and re-layouts  7.48 us

profile of v1, /device:TPU:1, one launch (start us, length us, event | category | flops | bytes accessed | tf_op | source)
XLA Modules:
  0.0 117.0 jit_solution(4879392804618137542)
XLA Ops:
  0.6 108.9 %shard_map.76 = (f32[8,64]{1,0:T(8,128)}, bf16[5,256,384]{2,1,0:T(8,128)(2,1)}, bf16[768,2048]{1,0:T(8,128)(2,1)}) custom-call(bf16[64,4096]{1,0:T(8,128)(2,1)} %g_hbm.1, s32[8,64]{1,0:T(8,128)} %bitcast.16, bf16[8,64]{1,0:T(8,128)(2,1)} %bitcast.17, bf16[5,256,384]{2,1,0:T(8,128)(2,1)} %bitcast.15, bf16[768,2048]{1,0:T(8,128)(2,1)} %bitcast.14), custom_call_target="tpu_custom_call" | custom-call | flops 15000000512 | bytes 10000000 | tf_op jit(solution)/shard_map/pallas_call | solution.py:429
  109.5 1.3 %copy.11 = f32[64,8]{0,1:T(8,128)} copy(f32[64,8]{0,1:T(8,128)} %bitcast.13) | data formatting | bytes 4096
  110.8 2.2 %copy.12 = bf16[1,256,5,384]{3,1,2,0:T(8,128)(2,1)} copy(bf16[1,256,5,384]{3,1,2,0:T(8,128)(2,1)} %bitcast.12) | data formatting | bytes 1966080
  113.1 4.0 %copy.13 = bf16[1,768,2048]{2,1,0:T(8,128)(2,1)} copy(bf16[1,768,2048]{2,1,0:T(8,128)(2,1)} %bitcast.11) | data formatting | bytes 6291456

commit v2 on v1

--- a/solution.py
+++ b/solution.py
@@ -44,8 +44,8 @@
     g_hbm, ids_ref, gates_ref, h_hbm, w_hbm,
     dgate_ref, dh_hbm, dw_hbm,
     tok, send, recv, pick, w_v, uacc, h_raw, h_all, scaled_t, dw_v, uex, dh_v, gate_col,
-    idx_mine, idx_other, meta_s, meta_r, code, gate_g, gm_s, gm_r, gp_s, gp_r, g2_s, g2_r, look, zmask,
-    sem_h, sem_w, sem_loc, swap_s, swap_r, idx_sem, hx_sem, meta_ss, meta_rs,
+    idx_s, idx_r, code, gate_g, gm_s, gm_r, gp_s, gp_r, g2_s, g2_r, look, zmask,
+    sem_h, sem_w, sem_loc, swap_s, swap_r, idx_ss, idx_rs, hx_sem, first_s, first_r,
     z_s, z_r, xy_s, xy_r, gm_ss, gm_rs, ex_s, ex_r, gp_ss, gp_rs, g2_ss, g2_rs, dw_sem, dh_sem,
 ):
     z = lax.axis_index("group")
@@ -92,6 +92,30 @@
         pl.semaphore_signal(barrier, 1, device_id=dev, device_id_type=MESH)
     pl.semaphore_wait(barrier, len(partners))
 
+    line = [sibling]
+    for d in range(1, NZ):
+        line.append(((z + d) % NZ, f))
+        line.append(((z + d) % NZ, p * 2 + other))
+
+    lanes16 = iota((16, 128), 1)
+    both = jnp.concatenate([ids_ref[...].astype(F32), gates_ref[...].astype(F32)], axis=0)
+    twice = jnp.concatenate([both, both], axis=1)
+    idx_s[...] = jnp.where(lanes16 // TOK == core, twice, 0.0)
+    idxs = []
+    for i, dev in enumerate(line):
+        cp = remote(idx_s, idx_r.at[z, core], idx_ss.at[i], idx_rs.at[i], dev)
+        cp.start()
+        idxs.append(cp)
+
+    first_cols = pl.ds(0, WIDTHS[0])
+    for d in range(1, NZ):
+        for to_core in (0, 1):
+            remote(
+                g_hbm.at[:, pl.ds(to_core * HALF_D, WIDTHS[0])],
+                tok.at[z, core, :, first_cols], first_s, first_r,
+                ((z + d) % NZ, p * 2 + to_core),
+            ).start()
+
     swaps = []
     for k in range(K):
         cols = pl.ds(STARTS[k], WIDTHS[k])
@@ -99,19 +123,11 @@
             g_hbm.at[:, pl.ds(pl.multiple_of(other * HALF_D + STARTS[k], 128), WIDTHS[k])],
             tok.at[z, core, :, cols], swap_s.at[k], swap_r.at[k], sibling,
         )
+        cp.start()
         swaps.append(cp)
-    swaps[0].start()
-
-    lanes16 = iota((16, 128), 1)
-    both = jnp.concatenate([ids_ref[...].astype(F32), gates_ref[...].astype(F32)], axis=0)
-    twice = jnp.concatenate([both, both], axis=1)
-    idx_mine[...] = jnp.where(lanes16 // TOK == core, twice, 0.0)
-    idx_cp = remote(idx_mine, idx_other, idx_sem.at[0], idx_sem.at[1], sibling)
-    idx_cp.start()
-    for k in range(1, K):
-        swaps[k].start()
     hx_cp = remote(h_hbm, h_raw.at[core], hx_sem.at[0], hx_sem.at[1], sibling)
     hx_cp.start()
+    idx_r[z, core] = idx_s[...]
 
     def ring(k, hop, way):
         sign = 1 if way == 0 else -1
@@ -145,74 +161,62 @@
         arrived(k, 3, 1 - k % 2)
         arrived(k, 4, k % 2)
 
-    hop1(0)
-
-    idx_cp.wait_recv()
-    table = idx_mine[...] + idx_other[...]
-    expert = iota((EXPERTS, 128), 0).astype(F32)
-    named = jnp.zeros((EXPERTS, 128), F32)
-    by_expert = jnp.zeros((EXPERTS, 128), F32)
-    for k in range(TOP):
-        hit = expert == table[k : k + 1]
-        named = named + jnp.where(hit, 1.0, 0.0)
-        by_expert = by_expert + jnp.where(hit, table[TOP + k : TOP + k + 1], 0.0)
+    for k in range(1, 5):
+        hop1(k)
+
+    for cp in idxs:
+        cp.wait_recv()
     before = iota((128, 128), 0)
     after = iota((128, 128), 1)
     upper = jnp.where((before < after) & (before // TOK == after // TOK), 1.0, 0.0).astype(BF16)
-    rank = nn(named.astype(BF16), upper)
-    rank_or = jnp.where(named > 0, rank, DEAD).astype(BF16)
-    meta_s[:, 0:16] = rank_or.reshape(NZ, NP, 128)
-    meta_s[:, 16:32] = by_expert.astype(BF16).reshape(NZ, NP, 128)
-    metas = []
-    for d in range(1, NZ):
-        to = (z + d) % NZ
-        cp = remote(meta_s.at[to], meta_r.at[z], meta_ss.at[d - 1], meta_rs.at[d - 1], (to, f))
-        cp.start()
-        metas.append(cp)
-    meta_r[z] = meta_s[z]
-
-    hop1(1)
-    hop23(0, 2)
-
-    lane_l = iota((128, 128), 0)
-    sub8 = iota((8, 128), 0)
-    for k in range(TOP):
-        ids_k = table[k : k + 1]
-        rank_k = jnp.sum(jnp.where(expert == ids_k, rank, 0.0), axis=0, keepdims=True)
-        ids_i = ids_k.astype(jnp.int32)
-        place = (ids_i % NP) * CAP + rank_k.astype(jnp.int32)
-        look[:, k * 128 : (k + 1) * 128] = jnp.where(lane_l == place, 1.0, 0.0).astype(BF16)
-        zmask[:, k * 128 : (k + 1) * 128] = jnp.where(sub8 == ids_i // NP, 1.0, 0.0)
-
-    hop1(2)
-    hop23(1, 2)
-    hop23(0, 3)
-
-    for cp in metas:
-        cp.wait_recv()
+    plane_expert = (z * NP + iota((NP, 128), 0)).astype(F32)
     for j in range(NZ):
+        tab = idx_r[j, 0] + idx_r[j, 1]
+        named = jnp.zeros((NP, 128), F32)
+        by_expert = jnp.zeros((NP, 128), F32)
+        for k in range(TOP):
+            hit = plane_expert == tab[k : k + 1]
+            named = named + jnp.where(hit, 1.0, 0.0)
+            by_expert = by_expert + jnp.where(hit, tab[TOP + k : TOP + k + 1], 0.0)
+        rank = nn(named.astype(BF16), upper)
         lane_src = (j * 128 + iota((NP, 128), 1)) // TOK
-        code[:, j * 128 : (j + 1) * 128] = meta_r[j, 0:16].astype(F32) + 8.0 * lane_src.astype(F32)
-        gate_g[:, j * 128 : (j + 1) * 128] = meta_r[j, 16:32]
+        coded = jnp.where(named > 0, rank + 8.0 * lane_src.astype(F32), DEAD)
+        code[:, j * 128 : (j + 1) * 128] = coded
+        gate_g[:, j * 128 : (j + 1) * 128] = by_expert.astype(BF16)
     row = iota((ROWS, 1024), 0)
     target = (row // SRC + 8 * (row % SRC)).astype(F32)
 
     @pl.loop(0, NP)
     def _(e):
-        chosen = jnp.where(code[pl.ds(e, 1), :] == target, 1.0, 0.0).astype(BF16)
-        pick[e] = chosen
-        gm = nt(gate_g[...], chosen)
-        gm_s[e] = jnp.concatenate([gm, jnp.zeros((NP, 128 - ROWS), F32)], axis=1).astype(BF16)
-
-    hop1(3)
-    hop23(2, 2)
-    hop23(1, 3)
-    hop4(0)
-
-    for i in range(1, NP):
-        to = plane(i)
-        remote(gm_s.at[to], gm_r.at[p], gm_ss, gm_rs, (z, to * 2 + core)).start()
-    gm_r[p] = gm_s[p]
+        pick[e] = jnp.where(code[pl.ds(e, 1), :] == target, 1.0, 0.0).astype(BF16)
+
+    def look_task():
+        table = idx_r[z, 0] + idx_r[z, 1]
+        expert = iota((EXPERTS, 128), 0).astype(F32)
+        named = jnp.zeros((EXPERTS, 128), F32)
+        for k in range(TOP):
+            named = named + jnp.where(expert == table[k : k + 1], 1.0, 0.0)
+        rank = nn(named.astype(BF16), upper)
+        lane_l = iota((128, 128), 0)
+        sub8 = iota((8, 128), 0)
+        for k in range(TOP):
+            ids_k = table[k : k + 1]
+            rank_k = jnp.sum(jnp.where(expert == ids_k, rank, 0.0), axis=0, keepdims=True)
+            ids_i = ids_k.astype(jnp.int32)
+            place = (ids_i % NP) * CAP + rank_k.astype(jnp.int32)
+            look[:, k * 128 : (k + 1) * 128] = jnp.where(lane_l == place, 1.0, 0.0).astype(BF16)
+            zmask[:, k * 128 : (k + 1) * 128] = jnp.where(sub8 == ids_i // NP, 1.0, 0.0)
+
+    def send_gates():
+        @pl.loop(0, NP)
+        def _(e):
+            gm = nt(gate_g[...], pick[e])
+            gm_s[e] = jnp.concatenate([gm, jnp.zeros((NP, 128 - ROWS), F32)], axis=1).astype(BF16)
+
+        for i in range(1, NP):
+            to = plane(i)
+            remote(gm_s.at[to], gm_r.at[p], gm_ss, gm_rs, (z, to * 2 + core)).start()
+        gm_r[p] = gm_s[p]
 
     def select(k):
         cols = pl.ds(STARTS[k], WIDTHS[k])
@@ -287,47 +291,63 @@
 
         pltpu.make_async_copy(dw_v.at[:, cols], dw_hbm.at[:, cols], dw_sem.at[k]).start()
 
-    for t in range(4, K + 6):
-        if t < K:
-            hop1(t)
-        if t - 1 < K:
-            hop23(t - 1, 2)
-        if t - 2 < K:
-            hop23(t - 2, 3)
-        if t - 3 < K:
-            hop4(t - 3)
-        if t - 4 < K:
-            gathered(t - 4)
-            select(t - 4)
-        if t == 4:
-            hidden_task()
-        if t == 5:
-            gate_task()
-            w_in.wait()
-        if t >= 6:
-            take_u(t - 6)
-            if t - 6 < K - 1:
-                take_w(t - 6)
+    def last_u(k):
+        cols = pl.ds(STARTS[k], WIDTHS[k])
+        w = WIDTHS[k]
+        wait_for(recv.at[:, pl.ds(0, NP - 1), :, cols], xy_r.at[k])
+        lane_t = iota((256, 128), 1)
+        terms = jnp.zeros((256, 128), F32)
+        for c in range(CAP):
+            u = uacc[c] + nt(recv[c, :, :, cols].reshape(256, w), w_v[:, cols])
+            uacc[c] = u
+            exs[c].start()
+            part = jnp.sum(u * h_all[c].astype(F32), axis=1, keepdims=True)
+            terms = terms + jnp.where(lane_t == p * CAP + c, part, 0.0)
+        gp_s[...] = terms.reshape(NP, SRC, 128)
+        for i in range(1, NP):
+            to = plane(i)
+            remote(gp_s.at[to], gp_r.at[p], gp_ss, gp_rs, (z, to * 2 + core)).start()
+        gp_r[p] = gp_s[p]
 
     exs = []
-    lane_t = iota((256, 128), 1)
-    terms = jnp.zeros((256, 128), F32)
     for c in range(CAP):
         cp = remote(
             uacc.at[c, :, pl.ds(pl.multiple_of(other * HALF_H, 128), HALF_H)], uex.at[c],
             ex_s.at[c], ex_r.at[c], sibling,
         )
-        cp.start()
         exs.append(cp)
-    for c in range(CAP):
-        part = jnp.sum(uacc[c] * h_all[c].astype(F32), axis=1, keepdims=True)
-        terms = terms + jnp.where(lane_t == p * CAP + c, part, 0.0)
-    gp_s[...] = terms.reshape(NP, SRC, 128)
-    for i in range(1, NP):
-        to = plane(i)
-        remote(gp_s.at[to], gp_r.at[p], gp_ss, gp_rs, (z, to * 2 + core)).start()
-    gp_r[p] = gp_s[p]
-
+
+    for k in range(1, 4):
+        hop23(k, 2)
+    locals_[0].wait()
+    swaps[0].wait_recv()
+    wait_for(tok.at[pl.ds(0, NZ - 1), :, :, first_cols], first_r)
+    select(0)
+    hop23(1, 3)
+    hop23(2, 3)
+    send_gates()
+    hop4(1)
+    hidden_task()
+    look_task()
+    for t in range(1, K + 2):
+        if t < K:
+            gathered(t)
+            select(t)
+        if t + 1 < K:
+            hop4(t + 1)
+        if t + 2 < K:
+            hop23(t + 2, 3)
+        if t + 3 < K:
+            hop23(t + 3, 2)
+        if t + 4 < K:
+            hop1(t + 4)
+        if t == 1:
+            gate_task()
+            w_in.wait()
+        if t >= 2 and t - 2 < K - 1:
+            take_u(t - 2)
+            take_w(t - 2)
+    last_u(K - 1)
     take_w(K - 1)
 
     def finish_hidden(c):
@@ -337,8 +357,6 @@
         dh_v[c] = nn(back, dh).astype(BF16)
         pltpu.make_async_copy(dh_v.at[c], dh_hbm.at[c], dh_sem.at[c]).start()
 
-    for c in range(CAP):
-        finish_hidden(c)
 
     wait_for(gp_r.at[pl.ds(0, NP - 1)], gp_rs)
     total = jnp.sum(gp_r[...], axis=0)
@@ -358,6 +376,8 @@
             cp.start()
             g2.append(cp)
     g2_r[core, z] = g2_s[z * 2 + core]
+    for c in range(CAP):
+        finish_hidden(c)
     for cp in g2:
         cp.wait_recv()
     summed = g2_r[0] + g2_r[1]
@@ -368,25 +388,47 @@
     rest = terms8 - hi.astype(F32)
     mid = rest.astype(BF16)
     low = (rest - mid.astype(F32)).astype(BF16)
+    got = nn(jnp.concatenate([hi, mid, low], axis=0), look[...])
+    line_g = jnp.sum((got[0:8] + got[8:16] + got[16:24]) * zmask[...], axis=0, keepdims=True)
     for k in range(TOP):
-        lk = look[:, k * 128 : (k + 1) * 128]
-        got = nn(hi, lk) + nn(mid, lk) + nn(low, lk)
-        line = jnp.sum(got * zmask[:, k * 128 : (k + 1) * 128], axis=0, keepdims=True)
-        dgate_ref[k : k + 1, :] = jnp.where(core == 0, line[:, 0:TOK], line[:, TOK:])
-
-    idx_cp.wait_send()
+        here = line_g[:, k * 128 : (k + 1) * 128]
+        dgate_ref[k : k + 1, :] = jnp.where(core == 0, here[:, 0:TOK], here[:, TOK:])
+
     hx_cp.wait_send()
-    for cp in swaps + metas + exs + g2:
+    for cp in swaps + idxs + exs + g2:
         cp.wait_send()
     for k in range(K):
         cols = pl.ds(STARTS[k], WIDTHS[k])
-        wait_for(tok.at[pl.ds(0, NZ - 1), :, :, cols], z_s.at[k])
+        wait_for(tok.at[pl.ds(0, NZ - 1), :, :, cols], z_s.at[k] if k else first_s)
         wait_for(recv.at[:, pl.ds(0, NP - 1), :, cols], xy_s.at[k])
         pltpu.make_async_copy(dw_v.at[:, cols], dw_hbm.at[:, cols], dw_sem.at[k]).wait()
     for c in range(CAP):
         pltpu.make_async_copy(dh_v.at[c], dh_hbm.at[c], dh_sem.at[c]).wait()
     wait_for(gm_r.at[pl.ds(0, NP - 1)], gm_ss)
     wait_for(gp_r.at[pl.ds(0, NP - 1)], gp_ss)
+
+
+def copies(dg_in, dh_in, dw_in, dg_out, dh_out, dw_out, dg_v, dh_v, dw_v, sems):
+    parts = []
+    for i in range(8):
+        rows = pl.ds(i * (H // 8), H // 8)
+        parts.append((dw_in.at[rows], dw_v.at[rows], dw_out.at[rows]))
+    for i in range(CAP):
+        parts.append((dh_in.at[i], dh_v.at[i], dh_out.at[i]))
+    parts.append((dg_in, dg_v, dg_out))
+    loads = []
+    for i, (src, mid, _) in enumerate(parts):
+        cp = pltpu.make_async_copy(src, mid, sems.at[0, i])
+        cp.start()
+        loads.append(cp)
+    stores = []
+    for i, (_, mid, dst) in enumerate(parts):
+        loads[i].wait()
+        cp = pltpu.make_async_copy(mid, dst, sems.at[1, i])
+        cp.start()
+        stores.append(cp)
+    for cp in stores:
+        cp.wait()
 
 
 def local(grad_out, expert_ids, gates, hidden_saved, w_down):
@@ -409,9 +451,7 @@
         vm((CAP, 256, HALF_H), BF16),
         vm((CAP, 256, 128), F32),
         vm((16, 128), F32),
-        vm((16, 128), F32),
-        vm((NZ, 32, 128), BF16),
-        vm((NZ, 32, 128), BF16),
+        vm((NZ, 2, 16, 128), F32),
         vm((NP, 1024), F32),
         vm((NP, 1024), BF16),
         vm((NP, NP, 128), BF16),
@@ -422,17 +462,18 @@
         vm((2, NZ, 8, 128), F32),
         vm((128, TOP * 128), BF16),
         vm((8, TOP * 128), F32),
-        dma, dma, dma((K,)), dma((K,)), dma((K,)), dma((2,)), dma((2,)), dma((7,)), dma((7,)),
+        dma, dma, dma((K,)), dma((K,)), dma((K,)), dma((15,)), dma((15,)), dma((2,)), dma, dma,
         dma((K,)), dma((2, 4, K)), dma((K,)), dma((K,)), dma, dma, dma((CAP,)), dma((CAP,)),
         dma, dma, dma((15,)), dma((15,)), dma((K,)), dma((CAP,)),
     ]
-    d_gate, d_hidden, d_weight = pl.pallas_call(
+    shapes = (
+        jax.ShapeDtypeStruct((TOP, TOK), F32),
+        jax.ShapeDtypeStruct((CAP, 256, HALF_H), BF16),
+        jax.ShapeDtypeStruct((H, HALF_D), BF16),
+    )
+    results = pl.pallas_call(
         kernel,
-        out_shape=(
-            jax.ShapeDtypeStruct((TOP, TOK), F32),
-            jax.ShapeDtypeStruct((CAP, 256, HALF_H), BF16),
-            jax.ShapeDtypeStruct((H, HALF_D), BF16),
-        ),
+        out_shape=shapes,
         in_specs=[anywhere, in_vmem, in_vmem, anywhere, anywhere],
         out_specs=(in_vmem, anywhere, anywhere),
         scratch_shapes=scratch,
@@ -443,6 +484,18 @@
             flops=15 * 10**9, bytes_accessed=10 * 10**6, transcendentals=0
         ),
     )(grad_out, expert_ids.T, gates.T, jnp.transpose(hidden_saved[0], (1, 0, 2)), w_down[0])
+    d_gate, d_hidden, d_weight = pl.pallas_call(
+        copies,
+        out_shape=shapes,
+        in_specs=[anywhere] * 3,
+        out_specs=(anywhere,) * 3,
+        scratch_shapes=[
+            vm((TOP, TOK), F32),
+            vm((CAP, 256, HALF_H), BF16),
+            vm((H, HALF_D), BF16),
+            dma((2, 14)),
+        ],
+    )(*results)
     return d_gate.T, jnp.transpose(d_hidden, (1, 0, 2))[None], d_weight[None]
 
 

time: 117 us -> 114 us (0.974)
  local copies, waits for them, and re-layouts: 7.48 us -> 0 us
  Pallas kernels: 109 us -> 114 us
    unnamed x3 -> x0, local copies, waits for them, and re-layouts: 7.48 us -> none
    pallas_call x1 -> x2, Pallas kernels: 109 us -> 114 us  [the longest x1 110 us: local(): pl.pallas_call(kernel, out_shape=shapes, in_specs=[anywhere, in_vmem, in_...]
where the time goes in v2:
time: 114 us
  Pallas kernels  114 us (100%)
    pallas_call x1, Pallas kernels, local(): pl.pallas_call(kernel, out_shape=shapes, in_specs=[anywhere, in_vmem, in_...  110 us
    pallas_call x1, Pallas kernels, local(): pl.pallas_call(copies, out_shape=shapes, in_specs=[anywhere] * 3, out_spe...  3.6 us

profile of v2, /device:TPU:1, one launch (start us, length us, event | category | flops | bytes accessed | tf_op | source)
XLA Modules:
  0.0 114.3 jit_solution(5275951746753665456)
XLA Ops:
  0.6 110.0 %shard_map.76 = (f32[8,64]{1,0:T(8,128)}, bf16[5,256,384]{2,1,0:T(8,128)(2,1)}, bf16[768,2048]{1,0:T(8,128)(2,1)}) custom-call(bf16[64,4096]{1,0:T(8,128)(2,1)} %g_hbm.1, s32[8,64]{1,0:T(8,128)} %bitcast.15, bf16[8,64]{1,0:T(8,128)(2,1)} %bitcast.17, bf16[5,256,384]{2,1,0:T(8,128)(2,1)} %bitcast.13, bf16[768,2048]{1,0:T(8,128)(2,1)} %bitcast.11), custom_call_target="tpu_custom_call" | custom-call | flops 15000000512 | bytes 10000000 | tf_op jit(solution)/shard_map/pallas_call | solution.py:474
  110.7 3.6 %shard_map.77 = (f32[8,64]{1,0:T(8,128)}, bf16[5,256,384]{2,1,0:T(8,128)(2,1)}, bf16[768,2048]{1,0:T(8,128)(2,1)}) custom-call(f32[8,64]{1,0:T(8,128)} %get-tuple-element.9.dg_in, bf16[5,256,384]{2,1,0:T(8,128)(2,1)} %get-tuple-element.10.dh_in, bf16[768,2048]{1,0:T(8,128)(2,1)} %get-tuple-element.11.dw_in), custom_call_target="tpu_custom_call" | custom-call | tf_op jit(solution)/shard_map/pallas_call | solution.py:487
